TPU v7x, 512 devices: a whole 4x4x16 slice. The times are simulated.
512 devices in a mesh: rep: 8 (over y, core), dp: 64 (over x, z).
Axes of the slice: x: 4, y: 4, z: 16, core: 2. Of those that a mesh axis runs over, the one named last changes fastest.
Arguments:
- grads: bfloat16 [8, 64, 1048576], P('rep', None, 'dp'), may hold values from -5 to 5
- owner: int32 [64], replicated, may hold values from 0 to 63, as said below
- left_root: bfloat16 [64, 3, 1024, 1024], P('dp', None, 'rep'), may hold values from -0.1875 to 0.1875
- right_root: bfloat16 [64, 3, 1024, 1024], P('dp', None, None, 'rep'), may hold values from -0.1875 to 0.1875
- momentum: float32 [64, 1048576], P(None, ('rep', 'dp')), may hold values from -6 to 6
- step: int32 [], replicated, may hold values from 1 to 3
Outputs:
- fresh: float32 [64, 1048576], P(None, ('rep', 'dp'))
- update: bfloat16 [64, 1048576], P(None, ('rep', 'dp'))
Inputs may be any that keep to these rules, and one draw needn't show every extreme that they name: `owner`: A quarter of the owners hold 3 blocks each, a quarter hold 1, the rest none; which owners and which blocks are drawn from the seed.
All inputs are finite; a program needn't handle non-finite values.
Results may differ from a plain program's by a relative error of at most 0.017.
Values may be sent and summed in bfloat16 or wider, within the bound.
A program may use at most 64 MiB of HBM per device.

v0:
```python
import jax
import jax.numpy as jnp
from jax import lax
from jax.sharding import PartitionSpec as P

BLOCK = 1024
MOST = 3


decay_rate = 0.5


def body(grads, owner, left_root, right_root, momentum, step):
    dp_size = lax.axis_size("dp")
    block_count = owner.shape[0]
    order = jnp.arange(block_count, dtype=jnp.int32)
    same = (owner[:, None] == owner[None, :]) & (order[None, :] < order[:, None])
    slot = jnp.sum(same.astype(jnp.int32), axis=1)
    target = jnp.arange(dp_size, dtype=jnp.int32)[None, :, None]
    place = jnp.arange(MOST, dtype=jnp.int32)[:, None, None]
    match = (owner[None, None, :] == target) & (slot[None, None, :] == place)
    present = jnp.any(match, axis=2)
    source_index = jnp.sum(jnp.where(match, order[None, None, :], 0), axis=2)
    source_index = jnp.where(present, source_index, block_count)
    partials = grads[0].astype(jnp.float32)
    summed = lax.psum(partials.astype(jnp.bfloat16), "rep")
    padded = jnp.concatenate([summed, jnp.zeros((1, summed.shape[1]), jnp.bfloat16)], axis=0)
    outgoing = jnp.take(padded, source_index, axis=0)
    arrived = lax.all_to_all(outgoing, "dp", split_axis=1, concat_axis=1, tiled=True)
    blocks = arrived.reshape(MOST, BLOCK, BLOCK)
    right_cols = right_root[0]
    left_rows = left_root[0]
    partial_cols = jnp.einsum(
        "sij,sjk->sik", blocks, right_cols, preferred_element_type=jnp.float32
    ).astype(jnp.bfloat16)
    direction_rows = jnp.einsum(
        "sij,sjk->sik",
        left_rows,
        lax.all_gather(partial_cols, "rep", axis=2, tiled=True),
        preferred_element_type=jnp.float32,
    ).astype(jnp.bfloat16)
    flat_rows = direction_rows.reshape(MOST, dp_size, -1)
    returned = lax.all_to_all(flat_rows, "dp", split_axis=1, concat_axis=1, tiled=True)
    mine = jnp.take(returned.reshape(MOST * dp_size, -1), slot * dp_size + owner, axis=0)
    fresh = decay_rate * momentum + (1.0 - decay_rate) * mine.astype(jnp.float32)
    factor = 1.0 - jnp.power(jnp.float32(decay_rate), step.astype(jnp.float32))
    update = (fresh / factor).astype(jnp.bfloat16)
    return (fresh, update)


def solution(mesh):
    return jax.shard_map(
        body,
        mesh=mesh,
        in_specs=(
            P("rep", None, "dp"),
            P(),
            P("dp", None, "rep", None),
            P("dp", None, None, "rep"),
            P(None, ("rep", "dp")),
            P(),
        ),
        out_specs=(P(None, ("rep", "dp")), P(None, ("rep", "dp"))),
        check_vma=False,
    )
```

profile of v0, /device:TPU:6, one launch (start us, length us, event | category | flops | bytes accessed | tf_op | source)
XLA Modules:
  0.0 659.2 jit_solution(1360023671764460814)
XLA Ops:
  7.2 0.0 copy-start
  7.2 0.0 all-reduce.3.cloned.1.call-start
  7.2 0.7 all-reduce.3.cloned.1.call-update
  7.9 0.0 all-gather.2.cloned.1.call-start
  8.0 0.9 convert_reduce_fusion
  8.9 0.7 iota_compare_fusion
  9.6 0.2 and_reduce_fusion
  9.7 0.1 fusion.3
  9.9 0.1 reshape.99
  10.0 0.1 copy.16
  10.1 85.9 %all-reduce.3.cloned.1.call-done = bf16[64,16384]{1,0:T(8,128)(2,1)} async-done(((bf16[64,16384]{1,0:T(8,128)(2,1)}), bf16[64,16384]{1,0:T(8,128)(2,1)}) %all-reduce.3.cloned.1.call-update) | async-done | bytes 2097168 | tf_op jit(solution)/shard_map/psum | solution.py:26
  96.0 1.7 concatenate.3
  97.7 7.2 %gather_fusion = bf16[192,16384]{1,0:T(8,128)(2,1)} fusion(bf16[65,16384]{1,0:T(8,128)(2,1)S(1)} %concatenate.3, s32[1024]{0:T(1024)S(1)} %pad_clamp_fusion.1), kind=kCustom, calls=%fused_computation | custom fusion | bytes 12583680 | tf_op jit(solution)/shard_map/jit(_take)/gather | solution.py:28
  104.9 16.7 %copy_select_fusion = bf16[3,64,16384]{2,0,1:T(4,128)(2,1)S(1)} fusion(bf16[3,64,16384]{2,1,0:T(8,128)(2,1)} %bitcast.17, pred[3,64]{0,1:T(8,128)(4,1)S(1)} %copy.16), kind=kLoop, calls=%fused_computation.2 | loop fusion | flops 3145728 | bytes 12583104 | tf_op jit(solution)/shard_map/jit(_take)/select_n | solution.py:28
  121.6 381.6 %all_to_all.10 = bf16[3,64,16384]{2,0,1:T(4,128)(2,1)S(1)} all-to-all(bf16[3,64,16384]{2,0,1:T(4,128)(2,1)S(1)} %copy_select_fusion), channel_id=1, replica_groups=mesh['rep'=8,'dp'=64] {'dp'}, dimensions={1} | all-to-all | bytes 12582912 | tf_op jit(solution)/shard_map/all_to_all | solution.py:29
  503.2 7.2 %copy.18 = bf16[3,64,16384]{2,1,0:T(8,128)(2,1)} copy(bf16[3,64,16384]{2,0,1:T(4,128)(2,1)S(1)} %all_to_all.10) | data formatting | bytes 12582912 | tf_op jit(solution)/shard_map/all_to_all | solution.py:29
  510.4 10.4 %reshape.94 = bf16[3,1024,1024]{2,1,0:T(8,128)(2,1)} reshape(bf16[3,64,16384]{2,1,0:T(8,128)(2,1)} %copy.18) | data formatting | bytes 12582912 | tf_op jit(solution)/shard_map/reshape | solution.py:30
  520.8 0.0 copy-done
  520.8 0.0 copy-start.3
  520.8 5.5 convolution_convert_fusion.1
  526.3 0.0 all-gather.2.cloned.1.call-update
  526.3 0.0 copy-start.2
  526.3 46.1 %all-gather.2.cloned.1.call-done = bf16[3,1024,1024]{2,1,0:T(8,128)(2,1)} async-done(((bf16[3,1024,128]{2,1,0:T(8,128)(2,1)}), bf16[3,1024,1024]{2,1,0:T(8,128)(2,1)}) %all-gather.2.cloned.1.call-update) | async-done | bytes 6291472 | tf_op jit(solution)/shard_map/all_gather | solution.py:39
  572.5 0.0 copy-done.3
  572.5 5.1 fusion
  577.6 0.0 copy-start.1
  577.6 0.3 copy.20
  577.9 0.3 reshape.95
  578.1 1.6 copy.21
  579.8 15.9 %all-to-all-start.1 = ((bf16[3,64,2048]{2,0,1:T(4,128)(2,1)}), bf16[3,64,2048]{2,0,1:T(4,128)(2,1)S(1)}, u32[]{:S(2)}, u32[]{:S(2)}) async-start(bf16[3,64,2048]{2,0,1:T(4,128)(2,1)} %copy.21), calls=%async_computation.1 | async-start | bytes 2097152 | tf_op jit(solution)/shard_map/all_to_all | solution.py:43
  596.4 0.0 copy-done.2
  596.4 53.6 %all-to-all-done.1 = bf16[3,64,2048]{2,0,1:T(4,128)(2,1)S(1)} async-done(((bf16[3,64,2048]{2,0,1:T(4,128)(2,1)}), bf16[3,64,2048]{2,0,1:T(4,128)(2,1)S(1)}, u32[]{:S(2)}, u32[]{:S(2)}) %all-to-all-start.1) | async-done | bytes 786464 | tf_op jit(solution)/shard_map/all_to_all | solution.py:43
  650.0 0.6 copy.22
  650.6 0.7 gather_fusion.1
  651.3 0.0 copy-done.1
  651.3 1.0 divide_convert_fusion
  (6 shorter events, 0.0 us)
Async XLA Ops:
  7.2 513.6 %copy-start = (bf16[1,3,1024,128]{3,2,1,0:T(8,128)(2,1)S(1)}, bf16[1,3,1024,128]{3,2,1,0:T(8,128)(2,1)}, u32[]{:S(2)}) copy-start(bf16[1,3,1024,128]{3,2,1,0:T(8,128)(2,1)} %param.9) | copy-start | bytes 2359300
  7.2 88.8 %all-reduce.3.cloned.1.call-start = ((), (), s32[]{:S(2)}) async-start(), calls=%async_computation.2 | async-start | bytes 4194304 | tf_op jit(solution)/shard_map/psum | solution.py:26
  7.9 564.6 %all-gather.2.cloned.1.call-start = ((), (), s32[]{:S(2)}) async-start(), calls=%async_computation.3 | async-start | bytes 7077888 | tf_op jit(solution)/shard_map/all_gather | solution.py:39
  520.8 51.7 %copy-start.3 = (bf16[1,3,128,1024]{3,2,1,0:T(8,128)(2,1)S(1)}, bf16[1,3,128,1024]{3,2,1,0:T(8,128)(2,1)}, u32[]{:S(2)}) copy-start(bf16[1,3,128,1024]{3,2,1,0:T(8,128)(2,1)} %param.8) | copy-start | bytes 2359300
  526.3 70.1 %copy-start.2 = (s32[64]{0:T(128)S(1)}, s32[64]{0:T(128)}, u32[]{:S(2)}) copy-start(s32[64]{0:T(128)} %param.7) | copy-start | bytes 772
  577.6 73.7 %copy-start.1 = (f32[64,2048]{1,0:T(8,128)S(1)}, f32[64,2048]{1,0:T(8,128)}, u32[]{:S(2)}) copy-start(f32[64,2048]{1,0:T(8,128)} %param.10) | copy-start | bytes 1572868
  579.8 70.2 %all-to-all-start.1 = ((bf16[3,64,2048]{2,0,1:T(4,128)(2,1)}), bf16[3,64,2048]{2,0,1:T(4,128)(2,1)S(1)}, u32[]{:S(2)}, u32[]{:S(2)}) async-start(bf16[3,64,2048]{2,0,1:T(4,128)(2,1)} %copy.21), calls=%async_computation.1 | async-start | bytes 2097152 | tf_op jit(solution)/shard_map/all_to_all | solution.py:43
Sparse Core Ops, SparseCore 0:
  10.4 85.5 all-reduce.2
  526.5 45.9 all-gather.1
where the time goes:
time: 660 us; the launch traced here: 659 us
  blocking collectives  382 us (58%)
  waiting for transfers between devices  186 us (28%)
  local copies, waits for them, and re-layouts  30.2 us (5%)
  other arithmetic  19.7 us (3%)
  starting transfers between devices  16 us (2%)
  between operations  14.9 us (2%)
  matrix products  10.6 us (2%)
    all_to_all x1, blocking collectives, body(): lax.all_to_all(outgoing, 'dp', split_axis=1, concat_axis=1, tiled=True)  382 us
    psum x1, waiting for transfers between devices, body(): summed = lax.psum(partials.astype(jnp.bfloat16), 'rep')  85.9 us
    all_to_all x1, waiting for transfers between devices, body(): lax.all_to_all(flat_rows, 'dp', split_axis=1, concat_axis=1, tiled=True)  53.6 us
    all_gather x1, waiting for transfers between devices, body(): lax.all_gather(partial_cols, 'rep', axis=2, tiled=True)  46.1 us
    select_n x2, other arithmetic, body(): outgoing = jnp.take(padded, source_index, axis=0)  16.8 us
    all_to_all x1, starting transfers between devices, body(): lax.all_to_all(flat_rows, 'dp', split_axis=1, concat_axis=1, tiled=True)  15.9 us
  transfers between devices with their start and end apart: 3, of which 3 were waited for; matrix products, arithmetic and copies ran while one was open for 0% of the time, Pallas kernels for 0%

commit v1 on v0

v1 whole, which is shorter than its diff:
```python
import functools

import jax
import jax.numpy as jnp
from jax import lax
from jax.experimental import pallas as pl
from jax.experimental.pallas import tpu as pltpu
from jax.sharding import PartitionSpec as P

BLOCK = 1024
MOST = 3
NX, NY, NZ, NR = 4, 4, 16, 8
NB = 64
FULL = NX * MOST
MESH = pl.DeviceIdType.MESH
Z_ORDER = (8, 7, 9, 6, 10, 5, 11, 4, 12, 3, 13, 2, 14, 1, 15)

decay_rate = 0.5


def tables_kernel(owner, blk, pos, ent, fin, most, per_line, per_plane):
    @pl.loop(0, NZ * FULL)
    def _(i):
        blk[i] = 0
        pos[i] = 0
        ent[i] = 0

    @pl.loop(0, NB)
    def _(i):
        per_line[i] = 0

    @pl.loop(0, NZ)
    def _(i):
        per_plane[i] = 0

    def place(b, top):
        line = owner[b]
        x, z = line // NZ, line % NZ
        s = per_line[line]
        e = per_plane[z]
        per_line[line] = s + 1
        per_plane[z] = e + 1
        blk[z * FULL + e] = b
        pos[z * FULL + x * MOST + s] = e
        ent[z * FULL + e] = s * NX + x
        fin[b] = z * 16 + e
        return jnp.maximum(top, e + 1)

    most[0] = lax.fori_loop(0, NB, place, jnp.int32(0))


def tables(owner):
    smem = pl.BlockSpec(memory_space=pltpu.SMEM)
    table = jax.ShapeDtypeStruct((NZ * FULL,), jnp.int32)
    return pl.pallas_call(
        tables_kernel,
        out_shape=(
            table,
            table,
            table,
            jax.ShapeDtypeStruct((NB,), jnp.int32),
            jax.ShapeDtypeStruct((1,), jnp.int32),
        ),
        in_specs=[smem],
        out_specs=(smem,) * 5,
        scratch_shapes=[pltpu.SMEM((NB,), jnp.int32), pltpu.SMEM((NZ,), jnp.int32)],
        name="tables",
    )(owner)


def step_kernel(
    cap, grads, left, right, blk, pos, ent, fin, out,
    gbuf, s_a, r_a, s_b, r_b, tsc, gt, s_z, r_z, s_x, gcol, lfull, rfull,
    s_w, r_w, s_e, r_e, s_q, r_q,
    load_sem, a1s, a1r, a2s, a2r, z1s, z1r, x1s, x1r, ns, nr, hs, hr, cs, cr, ws, wr, e1s, e1r, e2s, e2r,
):
    rep, dp = lax.axis_index("rep"), lax.axis_index("dp")
    y, c = rep // 2, rep % 2
    x, z = dp // NZ, dp % NZ

    def at(dx=0, dy=0, dz=0, dc=0):
        return (((y + dy) % NY) * 2 + (c + dc) % 2, ((x + dx) % NX) * NZ + (z + dz) % NZ)

    def remote(src, dst, send, recv, device):
        return pltpu.make_async_remote_copy(
            src_ref=src, dst_ref=dst, send_sem=send, recv_sem=recv, device_id=device, device_id_type=MESH
        )

    load_g = pltpu.make_async_copy(grads.at[0], gbuf, load_sem.at[0])
    load_g.start()
    load_l = pltpu.make_async_copy(left.at[0], lfull.at[:, rep], load_sem.at[1])
    load_l.start()
    load_r = pltpu.make_async_copy(right.at[0], rfull.at[:, rep], load_sem.at[2])
    load_r.start()

    with jax.named_scope("barrier"):
        barrier = pltpu.get_barrier_semaphore()
        peers = [at(dy=k // 2, dc=k % 2) for k in range(1, NR)]
        peers += [at(dx=k) for k in range(1, NX)]
        peers += [at(dz=k) for k in range(1, NZ)]
        for peer in peers:
            pl.semaphore_signal(barrier, inc=1, device_id=peer, device_id_type=MESH)
        pl.semaphore_wait(barrier, len(peers))

    def chunk(j, k, core):
        column = 8 * j + 2 * ((y + k) % NY) + core
        return gbuf[:, pl.ds(pl.multiple_of(128 * column, 128), 128)]

    a1 = [remote(s_a.at[k], r_a.at[k], a1s.at[k], a1r.at[k], at(dc=1)) for k in range(NY)]
    a2 = {k: remote(s_b.at[k], r_b.at[k], a2s.at[k], a2r.at[k], at(dy=k)) for k in (1, 2, 3)}
    with jax.named_scope("pair_sum"):
        load_g.wait()
        for k in (2, 1, 3, 0):

            @pl.loop(0, 16)
            def _(j, k=k):
                s_a[k, j] = chunk(j, k, 1 - c)

            a1[k].start()
        for k in (2, 1, 3):
            a1[k].wait_recv()

            @pl.loop(0, 16)
            def _(j, k=k):
                total = chunk(j, k, c).astype(jnp.float32) + r_a[k, j].astype(jnp.float32)
                s_b[k, j] = total.astype(jnp.bfloat16)

            a2[k].start()
    with jax.named_scope("y_sum"):
        a1[0].wait_recv()
        for k in (1, 2, 3):
            a2[k].wait_recv()

        @pl.loop(0, 16)
        def _(j):
            total = chunk(j, 0, c).astype(jnp.float32) + r_a[0, j].astype(jnp.float32)
            for k in (1, 2, 3):
                total += r_b[k, j].astype(jnp.float32)
            tsc[pl.ds(j, NB, stride=16), :] = total

        gt[...] = tsc[...].astype(jnp.bfloat16).reshape(NB, 16, 128)

    z1 = {k: remote(s_z.at[k], r_z.at[k], z1s.at[k], z1r.at[k], at(dz=k)) for k in range(1, NZ)}
    with jax.named_scope("to_plane"):
        for k in Z_ORDER + (0,):

            @pl.loop(0, cap)
            def _(e, k=k):
                tile = gt[blk[((z + k) % NZ) * FULL + e]]
                if k:
                    s_z[k, e] = tile
                else:
                    r_z[0, e] = tile

            if k:
                z1[k].start()

    def part(m, r, half=None):
        ref = (lfull if m < MOST else rfull).at[m % MOST, r]
        rows = 128 if m < MOST else 1024
        return ref if half is None else ref.at[pl.ds(half * (rows // 2), rows // 2)]

    def rep_of(dy, core):
        return ((y + dy) % NY) * 2 + core

    def near(m, up):
        return remote(part(m, rep), part(m, rep), ns.at[m, up], nr.at[m, up], at(dy=1 if up else 3))

    def near_in(m, up):
        r = rep_of(3 if up else 1, c)
        return remote(part(m, r), part(m, r), ns.at[m, up], nr.at[m, up], at(dy=1 if up else 3))

    def far(m, up):
        r = rep_of(3 if up else 1, c)
        return remote(part(m, r, up), part(m, r, up), hs.at[m, up], hr.at[m, up], at(dy=1 if up else 3))

    def far_in(m, up):
        r = rep_of(2, c)
        return remote(part(m, r, up), part(m, r, up), hs.at[m, up], hr.at[m, up], at(dy=1 if up else 3))

    def cross(m, k):
        r = rep_of(k, c)
        return remote(part(m, r), part(m, r), cs.at[m, k], cr.at[m, k], at(dc=1))

    def cross_in(m, k):
        r = rep_of(k, 1 - c)
        return remote(part(m, r), part(m, r), cs.at[m, k], cr.at[m, k], at(dc=1))

    def gather_start(ms):
        for m in ms:
            near(m, 1).start()
            near(m, 0).start()
            cross(m, 0).start()

    def gather_forward(ms):
        for m in ms:
            near_in(m, 1).wait_recv()
            far(m, 1).start()
            cross(m, 3).start()
            near_in(m, 0).wait_recv()
            far(m, 0).start()
            cross(m, 1).start()

    def gather_last(ms):
        for m in ms:
            far_in(m, 1).wait_recv()
            far_in(m, 0).wait_recv()
            cross(m, 2).start()

    def gather_done(ms):
        for m in ms:
            for k in range(NY):
                cross_in(m, k).wait_recv()

    lefts, rights = range(MOST), range(MOST, 2 * MOST)
    with jax.named_scope("left_start"):
        load_l.wait()
        gather_start(lefts)
    with jax.named_scope("left_forward"):
        gather_forward(lefts)
    load_r.wait()
    gather_start(rights)

    def x1(k, s):
        return remote(s_x.at[k, s], gcol.at[s, x], x1s.at[s, k], x1r.at[s, k], at(dx=k))

    def x1_in(k, s):
        return remote(s_x.at[k, s], gcol.at[s, (x + NX - k) % NX], x1s.at[s, k], x1r.at[s, k], at(dx=k))

    with jax.named_scope("at_plane"):
        for k in range(1, NZ):
            z1[k].wait_recv()
    with jax.named_scope("to_owner"):
        for s in range(MOST):
            for k in (2, 1, 3, 0):
                to = (x + k) % NX

                @pl.loop(0, NZ)
                def _(i, s=s, k=k, to=to):
                    tile = r_z[i, pos[z * FULL + to * MOST + s]]
                    rows = pl.ds(pl.multiple_of(16 * ((z + NZ - i) % NZ), 16), 16)
                    if k:
                        s_x[k, s, rows] = tile
                    else:
                        gcol[s, x, rows] = tile

                if k:
                    x1(k, s).start()
    with jax.named_scope("left_last"):
        gather_last(lefts)
        gather_done(lefts)

    def w1(k, s):
        r = rep_of(k // 2, (c + k) % 2)
        return remote(s_w.at[s, r], r_w.at[s, rep], ws.at[s, k], wr.at[s, k], at(dy=k // 2, dc=k % 2))

    def w1_in(k, s):
        r = rep_of(NY - k // 2, (c + k) % 2)
        return remote(s_w.at[s, r], r_w.at[s, r], ws.at[s, k], wr.at[s, k], at(dy=k // 2, dc=k % 2))

    with jax.named_scope("left_product"):
        for s in range(MOST):
            for k in range(1, NX):
                x1_in(k, s).wait_recv()
            g = gcol[s].reshape(BLOCK, 128)

            @pl.loop(0, 2)
            def _(h, s=s, g=g):
                rows = lfull[s, pl.ds(4 * h, 4)].reshape(512, BLOCK)
                w = jnp.dot(rows, g, preferred_element_type=jnp.float32)
                s_w[s, pl.ds(4 * h, 4)] = w.astype(jnp.bfloat16).reshape(4, 128, 128)

            for k in (4, 5, 2, 3, 6, 7, 1):
                w1(k, s).start()
            r_w[s, rep] = s_w[s, rep]
    with jax.named_scope("right_forward"):
        gather_forward(rights)
    with jax.named_scope("right_last"):
        gather_last(rights)
        gather_done(rights)

    def e1(k, s):
        return remote(s_e.at[s, (x + k) % NX], r_e.at[s * NX + x], e1s.at[s, k], e1r.at[s, k], at(dx=k))

    def e1_in(k, s):
        return remote(s_e.at[s, x], r_e.at[s * NX + (x + NX - k) % NX], e1s.at[s, k], e1r.at[s, k], at(dx=k))

    with jax.named_scope("right_product"):
        for s in range(MOST):
            for k in range(1, NR):
                w1_in(k, s).wait_recv()
            w = jnp.concatenate([r_w[s, r] for r in range(NR)], axis=1)
            for p in range(4):
                cols = jnp.concatenate([rfull[s, 2 * p], rfull[s, 2 * p + 1]], axis=1)
                d = jnp.dot(w, cols, preferred_element_type=jnp.float32)
                tsc[pl.ds(2 * p, 128, stride=8), :] = d[:, :128]
                tsc[pl.ds(2 * p + 1, 128, stride=8), :] = d[:, 128:]
            s_e[s] = tsc[...].astype(jnp.bfloat16).reshape(NX, 256, 128)
            for k in (2, 1, 3):
                e1(k, s).start()
            r_e[s * NX + x] = s_e[s, x]

    e2 = {k: remote(s_q.at[k], r_q.at[pl.ds(k * cap, cap)], e2s.at[k], e2r.at[k], at(dz=k)) for k in range(1, NZ)}
    with jax.named_scope("from_owner"):
        for s in range(MOST):
            for k in range(1, NX):
                e1_in(k, s).wait_recv()
    with jax.named_scope("from_plane"):
        for k in Z_ORDER + (0,):
            rows = pl.ds(pl.multiple_of(16 * ((z + k) % NZ), 16), 16)

            @pl.loop(0, cap)
            def _(e, k=k, rows=rows):
                tile = r_e[ent[z * FULL + e], rows]
                if k:
                    s_q[k, e] = tile
                else:
                    r_q[e] = tile

            if k:
                e2[k].start()
        for k in range(1, NZ):
            e2[k].wait_recv()
    with jax.named_scope("pick"):

        @pl.loop(0, NB)
        def _(b):
            v = fin[b]
            tile = r_q[((z + NZ - v // 16) % NZ) * cap + v % 16]
            tsc[pl.ds(pl.multiple_of(16 * b, 16), 16), :] = tile.astype(jnp.float32)

        for j in range(16):
            out[:, 128 * j : 128 * (j + 1)] = tsc[pl.ds(j, NB, stride=16), :].astype(jnp.bfloat16)

    with jax.named_scope("sends_done"):
        for k in range(NY):
            a1[k].wait_send()
        for k in (1, 2, 3):
            a2[k].wait_send()
        for k in range(1, NZ):
            z1[k].wait_send()
            e2[k].wait_send()
        for s in range(MOST):
            for k in range(1, NX):
                x1(k, s).wait_send()
                e1(k, s).wait_send()
            for k in range(1, NR):
                w1(k, s).wait_send()
        for m in range(2 * MOST):
            for up in range(2):
                near(m, up).wait_send()
                far(m, up).wait_send()
            for k in range(NY):
                cross(m, k).wait_send()


def directions(cap, cid, grads, left, right, blk, pos, ent, fin):
    bf16, f32, dma = jnp.bfloat16, jnp.float32, pltpu.SemaphoreType.DMA
    hbm = pl.BlockSpec(memory_space=pl.ANY)
    smem = pl.BlockSpec(memory_space=pltpu.SMEM)
    return pl.pallas_call(
        functools.partial(step_kernel, cap),
        out_shape=jax.ShapeDtypeStruct((NB, 2048), bf16),
        in_specs=[hbm] * 3 + [smem] * 4,
        out_specs=pl.BlockSpec(memory_space=pltpu.VMEM),
        scratch_shapes=[
            pltpu.VMEM((NB, 16384), bf16),
            pltpu.VMEM((NY, 16, NB, 128), bf16),
            pltpu.VMEM((NY, 16, NB, 128), bf16),
            pltpu.VMEM((NY, 16, NB, 128), bf16),
            pltpu.VMEM((NY, 16, NB, 128), bf16),
            pltpu.VMEM((BLOCK, 128), f32),
            pltpu.VMEM((NB, 16, 128), bf16),
            pltpu.VMEM((NZ, cap, 16, 128), bf16),
            pltpu.VMEM((NZ, cap, 16, 128), bf16),
            pltpu.VMEM((NX, MOST, 256, 128), bf16),
            pltpu.VMEM((MOST, NX, 256, 128), bf16),
            pltpu.VMEM((MOST, NR, 128, BLOCK), bf16),
            pltpu.VMEM((MOST, NR, BLOCK, 128), bf16),
            pltpu.VMEM((MOST, NR, 128, 128), bf16),
            pltpu.VMEM((MOST, NR, 128, 128), bf16),
            pltpu.VMEM((MOST, NX, 256, 128), bf16),
            pltpu.VMEM((MOST * NX, 256, 128), bf16),
            pltpu.VMEM((NZ, cap, 16, 128), bf16),
            pltpu.VMEM((NZ * cap, 16, 128), bf16),
            dma((3,)),
            dma((NY,)), dma((NY,)),
            dma((NY,)), dma((NY,)),
            dma((NZ,)), dma((NZ,)),
            dma((MOST, NX)), dma((MOST, NX)),
            dma((2 * MOST, 2)), dma((2 * MOST, 2)),
            dma((2 * MOST, 2)), dma((2 * MOST, 2)),
            dma((2 * MOST, NY)), dma((2 * MOST, NY)),
            dma((MOST, NR)), dma((MOST, NR)),
            dma((MOST, NX)), dma((MOST, NX)),
            dma((NZ,)), dma((NZ,)),
        ],
        compiler_params=pltpu.CompilerParams(
            collective_id=cid, has_side_effects=True, vmem_limit_bytes=48 * 2**20
        ),
        name=f"directions_{cap}",
    )(grads, left, right, blk, pos, ent, fin)


CAPS = (12,)


def body(grads, owner, left_root, right_root, momentum, step):
    blk, pos, ent, fin, most = tables(owner)
    args = (grads, left_root, right_root, blk, pos, ent, fin)
    if len(CAPS) == 1:
        mine = directions(CAPS[0], 0, *args)
    else:
        which = sum((most[0] > cap).astype(jnp.int32) for cap in CAPS[:-1])
        mine = lax.switch(which, [functools.partial(directions, cap, i) for i, cap in enumerate(CAPS)], *args)
    fresh = decay_rate * momentum + (1.0 - decay_rate) * mine.astype(jnp.float32)
    factor = 1.0 - jnp.power(jnp.float32(decay_rate), step.astype(jnp.float32))
    update = (fresh / factor).astype(jnp.bfloat16)
    return (fresh, update)


def solution(mesh):
    return jax.shard_map(
        body,
        mesh=mesh,
        in_specs=(
            P("rep", None, "dp"),
            P(),
            P("dp", None, "rep", None),
            P("dp", None, None, "rep"),
            P(None, ("rep", "dp")),
            P(),
        ),
        out_specs=(P(None, ("rep", "dp")), P(None, ("rep", "dp"))),
        check_vma=False,
    )
```

time: 660 us -> 164 us (0.25)
  blocking collectives: 382 us -> 0 us
  waiting for transfers between devices: 186 us -> 0 us
  Pallas kernels: 0 us -> 152 us
  local copies, waits for them, and re-layouts: 30.2 us -> 6.49 us
  other arithmetic: 19.7 us -> 0.97 us
  starting transfers between devices: 16 us -> 0 us
  between operations: 14.9 us -> 1.36 us
  matrix products: 10.6 us -> 0 us
    all_to_all x1 -> x0, blocking collectives: 382 us -> none  [body(): lax.all_to_all(outgoing, 'dp', split_axis=1, concat_axis=1, tiled=True)]
    pallas_call x0 -> x2, Pallas kernels: none -> 152 us  [the longest x1 148 us: directions(): pl.pallas_call(functools.partial(step_kernel, cap), out_shape=jax.ShapeDt...]
    psum x1 -> x0, waiting for transfers between devices: 85.9 us -> none  [body(): summed = lax.psum(partials.astype(jnp.bfloat16), 'rep')]
    all_to_all x1 -> x0, waiting for transfers between devices: 53.6 us -> none  [body(): lax.all_to_all(flat_rows, 'dp', split_axis=1, concat_axis=1, tiled=True)]
    all_gather x1 -> x0, waiting for transfers between devices: 46.1 us -> none  [body(): lax.all_gather(partial_cols, 'rep', axis=2, tiled=True)]
    select_n x2 -> x0, other arithmetic: 16.8 us -> none  [body(): outgoing = jnp.take(padded, source_index, axis=0)]
    all_to_all x1 -> x0, starting transfers between devices: 15.9 us -> none  [body(): lax.all_to_all(flat_rows, 'dp', split_axis=1, concat_axis=1, tiled=True)]
    reshape x3 -> x0, local copies, waits for them, and re-layouts: 12.3 us -> none  [the longest x1 10.4 us: body(): blocks = arrived.reshape(MOST, BLOCK, BLOCK)]
  transfers between devices with their start and end apart: 3 -> 0, of which waited for: 3 -> 0; matrix products, arithmetic and copies ran while one was open for 0% -> 0% of each run, Pallas kernels for 0% -> 0%
where the time goes in v1:
time: 164 us; the launch traced here: 161 us
  Pallas kernels  152 us (93%)
  local copies, waits for them, and re-layouts  6.49 us (4%)
    pallas_call x1, Pallas kernels, directions(): pl.pallas_call(functools.partial(step_kernel, cap), out_shape=jax.ShapeDt...  148 us
    unnamed x16, local copies, waits for them, and re-layouts  6.49 us
    pallas_call x1, Pallas kernels, tables(): pl.pallas_call(tables_kernel, out_shape=(table, table, table, jax.ShapeDt...  4.53 us

profile of v1, /device:TPU:6, one launch (start us, length us, event | category | flops | bytes accessed | tf_op | source)
XLA Modules:
  0.0 160.8 jit_solution(5105149690096725828)
XLA Ops:
  1.3 4.5 %tables.1 = (s32[192]{0:T(256)}, s32[192]{0:T(256)}, s32[192]{0:T(256)}, s32[64]{0:T(128)}, s32[1]{0:T(128)}) custom-call(s32[64]{0:T(128)} %owner.1), custom_call_target="tpu_custom_call" | custom-call | tf_op jit(solution)/shard_map/tables/pallas_call | solution.py:55
  5.9 0.0 copy-start
  5.9 1.6 copy-done
  7.5 0.0 copy-start.1
  7.5 1.1 copy-done.1
  8.6 0.0 copy-start.2
  8.6 1.1 copy-done.2
  9.7 0.0 copy-start.3
  9.7 0.7 copy-done.3
  10.4 0.0 copy-start.4
  10.4 0.7 copy-done.4
  11.1 0.0 copy-start.5
  11.1 0.7 copy-done.5
  11.7 0.0 copy-start.6
  11.7 0.6 copy-done.6
  12.4 0.0 copy-start.7
  12.4 147.5 %directions_12.1 = bf16[64,2048]{1,0:T(8,128)(2,1)S(1)} custom-call(bf16[1,64,16384]{2,1,0:T(8,128)(2,1)S(1)} %copy-done, bf16[1,3,128,1024]{3,2,1,0:T(8,128)(2,1)S(1)} %copy-done.1, bf16[1,3,1024,128]{3,2,1,0:T(8,128)(2,1)S(1)} %copy-done.2, s32[192]{0:T(256)S(1)} %copy-done.3, s32[192]{0:T(256)S(1)} %copy-done.4, s32[192]{0:T(256)S(1)} %copy-done.5, ...), custom_call_target="tpu_custom_call" | custom-call | tf_op jit(solution)/shard_map/directions_12/pallas_call | solution.py:361
  159.9 0.0 copy-done.7
  159.9 1.0 divide_convert_fusion
Async XLA Ops:
  5.9 1.6 copy-start
  7.5 1.1 copy-start.1
  8.6 1.1 copy-start.2
  9.7 0.7 copy-start.3
  10.4 0.7 copy-start.4
  11.1 0.7 copy-start.5
  11.7 0.6 copy-start.6
  12.4 147.5 %copy-start.7 = (f32[64,2048]{1,0:T(8,128)S(1)}, f32[64,2048]{1,0:T(8,128)}, u32[]{:S(2)}) copy-start(f32[64,2048]{1,0:T(8,128)} %param.10) | copy-start | bytes 1572868

commit v2 on v0

v2 whole, which is shorter than its diff:
```python
import functools

import jax
import jax.numpy as jnp
from jax import lax
from jax.experimental import pallas as pl
from jax.experimental.pallas import tpu as pltpu
from jax.sharding import PartitionSpec as P

BLOCK = 1024
MOST = 3
NX, NY, NZ, NR = 4, 4, 16, 8
NB = 64
MESH = pl.DeviceIdType.MESH
Z_ORDER = (8, 7, 9, 6, 10, 5, 11, 4, 12, 3, 13, 2, 14, 1, 15)
GATE = Z_ORDER[:7]


decay_rate = 0.5


def block_tables(cap, owner, tab):
    def spread(b, both):
        row, col = both
        return jnp.where(lane == b, owner[b], row), jnp.where(sub == b, owner[b], col)

    sub = lax.broadcasted_iota(jnp.int32, (NB, 128), 0)
    lane = lax.broadcasted_iota(jnp.int32, (NB, 128), 1)
    none = jnp.full((NB, 128), -1, jnp.int32)
    row, col = lax.fori_loop(0, NB, spread, (none, none))
    one = jnp.ones((NB, 128), jnp.int32)
    held = row >= 0
    same = held & (row == col)
    slot = jnp.sum(jnp.where(same & (lane < sub), one, 0), axis=1, keepdims=True)
    slot_row = jnp.sum(jnp.where(same & (sub < lane), one, 0), axis=0, keepdims=True)
    peers = held & ((row & 15) == (col & 15)) & (slot_row == slot) & (row < col)
    rank = jnp.sum(jnp.where(peers, one, 0), axis=1, keepdims=True)
    line = col[:, :1]
    x, z = line // NZ, line & 15
    j = jnp.where(slot == 0, x, jnp.minimum(rank, cap - 1))
    place = z * 16 + jnp.minimum(slot, MOST - 1) * 4 + j
    block = lax.broadcasted_iota(jnp.int32, (NB, 1), 0)
    index = lax.broadcasted_iota(jnp.int32, (NB, 256), 1)
    tab[...] = jnp.zeros_like(tab)
    rows = (
        (place, block, NB - 1),
        (z * 16 + slot * 4 + x, j, cap - 1),
        (place, x, NX - 1),
        (block, place, NZ * 16 - 1),
    )
    for i, (key, value, top) in enumerate(rows):
        tab[i : i + 1, :] = jnp.minimum(jnp.sum(jnp.where(index == key, value, 0), axis=0, keepdims=True), top)


def step_kernel(
    cap, grads, left, right, owner_in, out,
    owner, vtab, tab, gbuf, s_a, r_a, s_b, r_b, tsc, gt, s_z, r_z0, r_z1, r_z2, s_x, gfull, lrow, rfull,
    s_e, r_e0, r_e1, r_e2, s_q, r_q,
    load_sem, a1s, a1r, a2s, a2r, z1s, z1r, x1s, x1r, ns, nr, hs, hr, cs, cr, e1s, e1r, e2s, e2r,
):
    caps = (NX, cap, cap)
    starts = (0, NX, NX + cap)
    rep, dp = lax.axis_index("rep"), lax.axis_index("dp")
    y, c = rep // 2, rep % 2
    x, z = dp // NZ, dp % NZ

    def at(dx=0, dy=0, dz=0, dc=0):
        return (((y + dy) % NY) * 2 + (c + dc) % 2, ((x + dx) % NX) * NZ + (z + dz) % NZ)

    def remote(src, dst, send, recv, device):
        return pltpu.make_async_remote_copy(
            src_ref=src, dst_ref=dst, send_sem=send, recv_sem=recv, device_id=device, device_id_type=MESH
        )

    load_o = pltpu.make_async_copy(owner_in, owner, load_sem.at[3])
    load_o.start()
    load_g = pltpu.make_async_copy(grads.at[0], gbuf, load_sem.at[0])
    load_g.start()
    load_l = pltpu.make_async_copy(left.at[0], lrow, load_sem.at[1])
    load_l.start()
    load_r = pltpu.make_async_copy(right.at[0], rfull.at[:, rep], load_sem.at[2])
    load_r.start()

    barrier = pltpu.get_barrier_semaphore()
    peers = [at(dz=k) for k in Z_ORDER] + [at(dx=k) for k in (2, 1, 3)]
    peers += [at(dy=k) for k in (1, 2, 3)] + [at(dc=1)]
    for peer in peers:
        pl.semaphore_signal(barrier, inc=1, device_id=peer, device_id_type=MESH)

    links = {}
    loads = {"left": load_l, "right": load_r, "owner": load_o}

    def go(name, out, back):
        out.start()
        links[name] = [out, back, True, True]

    def arrive(*name):
        links[name][1].wait_recv()
        links[name][2] = False

    def left(*name):
        links[name][0].wait_send()
        links[name][3] = False

    def loaded(name):
        loads.pop(name).wait()

    def finish():
        for copy in loads.values():
            copy.wait()
        for out, back, due, sent in links.values():
            if due:
                back.wait_recv()
            if sent:
                out.wait_send()

    def chunk(j, k, core):
        column = 8 * j + 2 * ((y + k) % NY) + core
        return gbuf[:, pl.ds(pl.multiple_of(128 * column, 128), 128)]

    def part(m, r, half=None):
        if m < MOST:
            return rfull.at[m, r] if half is None else rfull.at[m, r, pl.ds(half * 512, 512)]
        return gfull.at[m - MOST, r] if half is None else gfull.at[m - MOST, r, pl.ds(2 * half, 2)]

    def rep_of(dy, core):
        return ((y + dy) % NY) * 2 + core

    def near(m):
        for up in (1, 0):

            def copy(r, up=up):
                return remote(part(m, r), part(m, r), ns.at[m, up], nr.at[m, up], at(dy=1 if up else 3))

            go(("near", m, up), copy(rep), copy(rep_of(3 if up else 1, c)))
        cross(m, 0)

    def far(m, up):
        def copy(r):
            return remote(part(m, r, up), part(m, r, up), hs.at[m, up], hr.at[m, up], at(dy=1 if up else 3))

        go(("far", m, up), copy(rep_of(3 if up else 1, c)), copy(rep_of(2, c)))

    def cross(m, k):
        def copy(core):
            r = rep_of(k, core)
            return remote(part(m, r), part(m, r), cs.at[m, k], cr.at[m, k], at(dc=1))

        go(("cross", m, k), copy(c), copy(1 - c))

    def forward(m):
        for up in (1, 0):
            arrive("near", m, up)
            far(m, up)
        cross(m, 3)
        cross(m, 1)

    def last(m):
        arrive("far", m, 1)
        arrive("far", m, 0)
        cross(m, 2)

    def whole(m):
        for k in range(NY):
            arrive("cross", m, k)

    with jax.named_scope("pair_pack"):
        load_g.wait()
        for k in (2, 1, 3, 0):

            @pl.loop(0, 16)
            def _(j, k=k):
                s_a[k, j] = chunk(j, k, 1 - c)

    with jax.named_scope("barrier"):
        pl.semaphore_wait(barrier, len(peers))

    with jax.named_scope("pair_sum"):
        for k in (2, 1, 3, 0):
            copy = remote(s_a.at[k], r_a.at[k], a1s.at[k], a1r.at[k], at(dc=1))
            go(("a1", k), copy, copy)
        loaded("right")
        near(0)
        for k in (2, 1, 3):
            arrive("a1", k)

            @pl.loop(0, 16)
            def _(j, k=k):
                total = chunk(j, k, c).astype(jnp.float32) + r_a[k, j].astype(jnp.float32)
                s_b[k, j] = total.astype(jnp.bfloat16)

            copy = remote(s_b.at[k], r_b.at[k], a2s.at[k], a2r.at[k], at(dy=k))
            go(("a2", k), copy, copy)

    with jax.named_scope("tables"):
        loaded("owner")
        block_tables(cap, owner, vtab)
        to_smem = pltpu.make_async_copy(vtab, tab, load_sem.at[4])
        to_smem.start()
        loads["tables"] = to_smem

    with jax.named_scope("y_sum"):
        arrive("a1", 0)
        for k in (1, 2, 3):
            arrive("a2", k)

        @pl.loop(0, 16)
        def _(j):
            total = chunk(j, 0, c).astype(jnp.float32) + r_a[0, j].astype(jnp.float32)
            for k in (1, 2, 3):
                total += r_b[k, j].astype(jnp.float32)
            tsc[pl.ds(j, NB, stride=16), :] = total

        gt[...] = tsc[...].astype(jnp.bfloat16).reshape(NB, 16, 128)
        loaded("tables")

    r_z, r_e = (r_z0, r_z1, r_z2), (r_e0, r_e1, r_e2)

    def to_plane(s):
        for k in Z_ORDER + (0,):

            @pl.loop(0, caps[s])
            def _(e, k=k):
                tile = gt[tab[0, ((z + k) % NZ) * 16 + 4 * s + e]]
                if k:
                    s_z[k, starts[s] + e] = tile
                else:
                    r_z[s][0, e] = tile

            if k:
                copy = remote(s_z.at[k, pl.ds(starts[s], caps[s])], r_z[s].at[k], z1s.at[s, k], z1r.at[s, k], at(dz=k))
                go(("z1", s, k), copy, copy)

    def to_owner(s):
        for k in range(1, NZ):
            arrive("z1", s, k)
        for k in (2, 1, 3, 0):
            to = (x + k) % NX

            @pl.loop(0, NZ)
            def _(i, k=k, to=to):
                tile = r_z[s][i, tab[1, z * 16 + 4 * s + to] if s else to]
                rows = pl.ds(pl.multiple_of(16 * ((z + NZ - i) % NZ), 16), 16)
                if k:
                    s_x[k, s, rows] = tile
                else:
                    gfull[s, rep, x, rows] = tile

            if k:

                def x1(to, k=k):
                    return remote(s_x.at[k, s], gfull.at[s, rep, to], x1s.at[s, k], x1r.at[s, k], at(dx=k))

                go(("x1", s, k), x1(x), x1((x + NX - k) % NX))

    def at_owner(s):
        for k in range(1, NX):
            arrive("x1", s, k)
        near(MOST + s)

    def products(s):
        whole(s)
        whole(MOST + s)
        w = []
        for p in range(4):
            cols = jnp.concatenate([gfull[s, 2 * p + i].reshape(BLOCK, 128) for i in range(2)], axis=1)
            w.append(jnp.dot(lrow[s], cols, preferred_element_type=jnp.float32).astype(jnp.bfloat16))
        w = jnp.concatenate(w, axis=1)
        for p in range(4):
            cols = jnp.concatenate([rfull[s, 2 * p], rfull[s, 2 * p + 1]], axis=1)
            d = jnp.dot(w, cols, preferred_element_type=jnp.float32)
            tsc[pl.ds(2 * p, 128, stride=8), :] = d[:, :128]
            tsc[pl.ds(2 * p + 1, 128, stride=8), :] = d[:, 128:]
        s_e[s] = tsc[...].astype(jnp.bfloat16).reshape(NX, NZ, 16, 128)
        for k in (2, 1, 3):

            def e1(to, come, k=k):
                return remote(s_e.at[s, to], r_e[s].at[come], e1s.at[s, k], e1r.at[s, k], at(dx=k))

            go(("e1", s, k), e1((x + k) % NX, x), e1(x, (x + NX - k) % NX))
        r_e[s][x] = s_e[s, x]

    def from_owner(s):
        for k in range(1, NX):
            arrive("e1", s, k)
        for k in Z_ORDER + (0,):

            @pl.loop(0, caps[s])
            def _(e, k=k):
                tile = r_e[s][tab[2, z * 16 + 4 * s + e] if s else e, (z + k) % NZ]
                if k:
                    s_q[k, starts[s] + e] = tile
                else:
                    r_q[0, starts[s] + e] = tile

            if k:
                mine = pl.ds(starts[s], caps[s])
                copy = remote(s_q.at[k, mine], r_q.at[k, mine], e2s.at[s, k], e2r.at[s, k], at(dz=k))
                go(("e2", s, k), copy, copy)

    def gate(s):
        for k in GATE:
            left("z1", s, k)

    with jax.named_scope("out"):
        to_plane(0)
        near(1)
        near(2)
        forward(0)
    with jax.named_scope("out_1"):
        gate(0)
        to_plane(1)
        forward(1)
        forward(2)
        to_owner(0)
    with jax.named_scope("out_2"):
        gate(1)
        to_plane(2)
        at_owner(0)
        for s in range(MOST):
            last(s)
    with jax.named_scope("gather_0"):
        to_owner(1)
        forward(3)
        at_owner(1)
        last(3)
    with jax.named_scope("product_0"):
        loaded("left")
        products(0)
    with jax.named_scope("gather_1"):
        to_owner(2)
        forward(4)
        at_owner(2)
        from_owner(0)
        last(4)
    with jax.named_scope("product_1"):
        products(1)
        forward(5)
        last(5)
        from_owner(1)
    with jax.named_scope("product_2"):
        products(2)
        from_owner(2)
    with jax.named_scope("at_shards"):
        for s in range(MOST):
            for k in range(1, NZ):
                arrive("e2", s, k)
    with jax.named_scope("pick"):

        @pl.loop(0, NB)
        def _(b):
            v = tab[3, b]
            place = v % 16
            tile = r_q[(z + NZ - v // 16) % NZ, place - (place // 8) * (NX - cap)]
            tsc[pl.ds(pl.multiple_of(16 * b, 16), 16), :] = tile.astype(jnp.float32)

        for j in range(16):
            out[:, 128 * j : 128 * (j + 1)] = tsc[pl.ds(j, NB, stride=16), :].astype(jnp.bfloat16)

    with jax.named_scope("sends_done"):
        finish()


def directions(cap, cid, grads, left, right, owner):
    bf16, f32, dma = jnp.bfloat16, jnp.float32, pltpu.SemaphoreType.DMA
    hbm = pl.BlockSpec(memory_space=pl.ANY)
    return pl.pallas_call(
        functools.partial(step_kernel, cap),
        out_shape=jax.ShapeDtypeStruct((NB, 2048), bf16),
        in_specs=[hbm] * 4,
        out_specs=pl.BlockSpec(memory_space=pltpu.VMEM),
        scratch_shapes=[
            pltpu.SMEM((NB,), jnp.int32),
            pltpu.VMEM((8, 256), jnp.int32),
            pltpu.SMEM((8, 256), jnp.int32),
            pltpu.VMEM((NB, 16384), bf16),
            pltpu.VMEM((NY, 16, NB, 128), bf16),
            pltpu.VMEM((NY, 16, NB, 128), bf16),
            pltpu.VMEM((NY, 16, NB, 128), bf16),
            pltpu.VMEM((NY, 16, NB, 128), bf16),
            pltpu.VMEM((BLOCK, 128), f32),
            pltpu.VMEM((NB, 16, 128), bf16),
            pltpu.VMEM((NZ, NX + 2 * cap, 16, 128), bf16),
            pltpu.VMEM((NZ, NX, 16, 128), bf16),
            pltpu.VMEM((NZ, cap, 16, 128), bf16),
            pltpu.VMEM((NZ, cap, 16, 128), bf16),
            pltpu.VMEM((NX, MOST, 256, 128), bf16),
            pltpu.VMEM((MOST, NR, NX, 256, 128), bf16),
            pltpu.VMEM((MOST, 128, BLOCK), bf16),
            pltpu.VMEM((MOST, NR, BLOCK, 128), bf16),
            pltpu.VMEM((MOST, NX, NZ, 16, 128), bf16),
            pltpu.VMEM((NX, NZ, 16, 128), bf16),
            pltpu.VMEM((NX, NZ, 16, 128), bf16),
            pltpu.VMEM((NX, NZ, 16, 128), bf16),
            pltpu.VMEM((NZ, NX + 2 * cap, 16, 128), bf16),
            pltpu.VMEM((NZ, NX + 2 * cap, 16, 128), bf16),
            dma((5,)),
            dma((NY,)), dma((NY,)),
            dma((NY,)), dma((NY,)),
            dma((MOST, NZ)), dma((MOST, NZ)),
            dma((MOST, NX)), dma((MOST, NX)),
            dma((2 * MOST, 2)), dma((2 * MOST, 2)),
            dma((2 * MOST, 2)), dma((2 * MOST, 2)),
            dma((2 * MOST, NY)), dma((2 * MOST, NY)),
            dma((MOST, NX)), dma((MOST, NX)),
            dma((MOST, NZ)), dma((MOST, NZ)),
        ],
        compiler_params=pltpu.CompilerParams(
            collective_id=cid, has_side_effects=True, vmem_limit_bytes=48 * 2**20
        ),
        name=f"directions_{cap}",
    )(grads, left, right, owner)


CAPS = (3, NX)


def body(grads, owner, left_root, right_root, momentum, step):
    lines = jnp.arange(NX * NZ, dtype=jnp.int32).reshape(NX, NZ, 1)
    held = jnp.sum((owner == lines).astype(jnp.int32), axis=2)
    most = jnp.max(jnp.sum((held > 1).astype(jnp.int32), axis=0))
    which = sum((most > cap).astype(jnp.int32) for cap in CAPS[:-1])
    branches = [functools.partial(directions, cap, i) for i, cap in enumerate(CAPS)]
    mine = lax.switch(which, branches, grads, left_root, right_root, owner)
    fresh = decay_rate * momentum + (1.0 - decay_rate) * mine.astype(jnp.float32)
    factor = 1.0 - jnp.power(jnp.float32(decay_rate), step.astype(jnp.float32))
    update = (fresh / factor).astype(jnp.bfloat16)
    return (fresh, update)


def solution(mesh):
    return jax.shard_map(
        body,
        mesh=mesh,
        in_specs=(
            P("rep", None, "dp"),
            P(),
            P("dp", None, "rep", None),
            P("dp", None, None, "rep"),
            P(None, ("rep", "dp")),
            P(),
        ),
        out_specs=(P(None, ("rep", "dp")), P(None, ("rep", "dp"))),
        check_vma=False,
    )
```

time: 660 us -> 119 us (0.18)
  blocking collectives: 382 us -> 0 us
  waiting for transfers between devices: 186 us -> 0 us
  Pallas kernels: 0 us -> 114 us
  local copies, waits for them, and re-layouts: 30.2 us -> 0.01 us
  other arithmetic: 19.7 us -> 2.5 us
  starting transfers between devices: 16 us -> 0 us
  between operations: 14.9 us -> 2.01 us
  matrix products: 10.6 us -> 0 us
    all_to_all x1 -> x0, blocking collectives: 382 us -> none  [body(): lax.all_to_all(outgoing, 'dp', split_axis=1, concat_axis=1, tiled=True)]
    pallas_call x0 -> x1, Pallas kernels: none -> 114 us  [directions(): pl.pallas_call(functools.partial(step_kernel, cap), out_shape=jax.ShapeDt...]
    psum x1 -> x0, waiting for transfers between devices: 85.9 us -> none  [body(): summed = lax.psum(partials.astype(jnp.bfloat16), 'rep')]
    all_to_all x1 -> x0, waiting for transfers between devices: 53.6 us -> none  [body(): lax.all_to_all(flat_rows, 'dp', split_axis=1, concat_axis=1, tiled=True)]
    all_gather x1 -> x0, waiting for transfers between devices: 46.1 us -> none  [body(): lax.all_gather(partial_cols, 'rep', axis=2, tiled=True)]
    select_n x2 -> x0, other arithmetic: 16.8 us -> none  [body(): outgoing = jnp.take(padded, source_index, axis=0)]
    all_to_all x1 -> x0, starting transfers between devices: 15.9 us -> none  [body(): lax.all_to_all(flat_rows, 'dp', split_axis=1, concat_axis=1, tiled=True)]
    reshape x3 -> x0, local copies, waits for them, and re-layouts: 12.3 us -> none  [the longest x1 10.4 us: body(): blocks = arrived.reshape(MOST, BLOCK, BLOCK)]
  transfers between devices with their start and end apart: 3 -> 0, of which waited for: 3 -> 0; matrix products, arithmetic and copies ran while one was open for 0% -> 0% of each run, Pallas kernels for 0% -> 0%
where the time goes in v2:
time: 119 us; the launch traced here: 118 us
  Pallas kernels  114 us (96%)
  other arithmetic  2.5 us (2%)
  between operations  2.01 us (2%)
    pallas_call x1, Pallas kernels, directions(): pl.pallas_call(functools.partial(step_kernel, cap), out_shape=jax.ShapeDt...  114 us

profile of v2, /device:TPU:6, one launch (start us, length us, event | category | flops | bytes accessed | tf_op | source)
XLA Modules:
  0.0 118.3 jit_solution(3669875856517986407)
XLA Ops:
  1.3 0.9 convert_reduce_fusion
  2.2 0.6 reduce_max.9
  3.5 0.0 copy-start
  3.5 113.7 %conditional.6 = (bf16[64,2048]{1,0:T(8,128)(2,1)S(1)}) conditional(s32[]{:T(128)} %clamp.3, (bf16[1,64,16384]{2,1,0:T(8,128)(2,1)}, bf16[1,3,128,1024]{3,2,1,0:T(8,128)(2,1)}, bf16[1,3,1024,128]{3,2,1,0:T(8,128)(2,1)}, s32[64]{0:T(128)}) %tuple.24, (bf16[1,64,16384]{2,1,0:T(8,128)(2,1)}, bf16[1,3,128,1024]{3,2,1,0:T(8,128)(2,1)}, ...), branch_computations={%region_3.0_spmd, %region_4.0_spmd} | conditional | bytes 8
  3.5 113.7 %directions_3.1 = bf16[64,2048]{1,0:T(8,128)(2,1)S(1)} custom-call(bf16[1,64,16384]{2,1,0:T(8,128)(2,1)} %get-tuple-element.25.grads, bf16[1,3,128,1024]{3,2,1,0:T(8,128)(2,1)} %get-tuple-element.26.left, bf16[1,3,1024,128]{3,2,1,0:T(8,128)(2,1)} %get-tuple-element.27.right, s32[64]{0:T(128)} %get-tuple-element.28.owner_in), custom_call_target="tpu_custom_call" | custom-call | tf_op jit(solution)/shard_map/cond/branch_0_fun/directions_3/pallas_call | solution.py:367
  117.3 0.0 copy-done
  117.3 1.0 divide_convert_fusion
  (2 shorter events, 0.0 us)
Async XLA Ops:
  3.5 113.8 %copy-start = (f32[64,2048]{1,0:T(8,128)S(1)}, f32[64,2048]{1,0:T(8,128)}, u32[]{:S(2)}) copy-start(f32[64,2048]{1,0:T(8,128)} %param.12) | copy-start | bytes 1572868

commit v3 on v2

--- a/solution.py
+++ b/solution.py
@@ -319,23 +319,23 @@
         at_owner(0)
         for s in range(MOST):
             last(s)
-    with jax.named_scope("gather_0"):
+    with jax.named_scope("gather"):
         to_owner(1)
         forward(3)
         at_owner(1)
+        to_owner(2)
         last(3)
+        forward(4)
+        at_owner(2)
     with jax.named_scope("product_0"):
         loaded("left")
         products(0)
-    with jax.named_scope("gather_1"):
-        to_owner(2)
-        forward(4)
-        at_owner(2)
+    with jax.named_scope("gather_2"):
+        last(4)
+        forward(5)
         from_owner(0)
-        last(4)
     with jax.named_scope("product_1"):
         products(1)
-        forward(5)
         last(5)
         from_owner(1)
     with jax.named_scope("product_2"):

time: 119 us -> 118 us (level)
  Pallas kernels: 114 us -> 112 us
    pallas_call x1, Pallas kernels: 114 us -> 112 us  [directions(): pl.pallas_call(functools.partial(step_kernel, cap), out_shape=jax.ShapeDt...]
where the time goes in v3:
time: 118 us; the launch traced here: 117 us
  Pallas kernels  112 us (95%)
  other arithmetic  2.5 us (2%)
  between operations  2.01 us (2%)
    pallas_call x1, Pallas kernels, directions(): pl.pallas_call(functools.partial(step_kernel, cap), out_shape=jax.ShapeDt...  112 us

profile of v3, /device:TPU:6, one launch (start us, length us, event | category | flops | bytes accessed | tf_op | source)
XLA Modules:
  0.0 116.9 jit_solution(9247794534894032192)
XLA Ops:
  1.3 0.9 convert_reduce_fusion
  2.2 0.6 reduce_max.9
  3.5 0.0 copy-start
  3.5 112.4 %conditional.6 = (bf16[64,2048]{1,0:T(8,128)(2,1)S(1)}) conditional(s32[]{:T(128)} %clamp.3, (bf16[1,64,16384]{2,1,0:T(8,128)(2,1)}, bf16[1,3,128,1024]{3,2,1,0:T(8,128)(2,1)}, bf16[1,3,1024,128]{3,2,1,0:T(8,128)(2,1)}, s32[64]{0:T(128)}) %tuple.24, (bf16[1,64,16384]{2,1,0:T(8,128)(2,1)}, bf16[1,3,128,1024]{3,2,1,0:T(8,128)(2,1)}, ...), branch_computations={%region_3.0_spmd, %region_4.0_spmd} | conditional | bytes 8
  3.5 112.4 %directions_3.1 = bf16[64,2048]{1,0:T(8,128)(2,1)S(1)} custom-call(bf16[1,64,16384]{2,1,0:T(8,128)(2,1)} %get-tuple-element.25.grads, bf16[1,3,128,1024]{3,2,1,0:T(8,128)(2,1)} %get-tuple-element.26.left, bf16[1,3,1024,128]{3,2,1,0:T(8,128)(2,1)} %get-tuple-element.27.right, s32[64]{0:T(128)} %get-tuple-element.28.owner_in), custom_call_target="tpu_custom_call" | custom-call | tf_op jit(solution)/shard_map/cond/branch_0_fun/directions_3/pallas_call | solution.py:367
  115.9 0.0 copy-done
  115.9 1.0 divide_convert_fusion
  (2 shorter events, 0.0 us)
Async XLA Ops:
  3.5 112.4 %copy-start = (f32[64,2048]{1,0:T(8,128)S(1)}, f32[64,2048]{1,0:T(8,128)}, u32[]{:S(2)}) copy-start(f32[64,2048]{1,0:T(8,128)} %param.12) | copy-start | bytes 1572868
